TPU v7x, 32 devices: a whole 2x2x4 slice. The times are simulated.
32 devices in a mesh: dp: 4 (over y, x), ctx: 8 (over z, core).
Axes of the slice: x: 2, y: 2, z: 4, core: 2. Of those that a mesh axis runs over, the one named last changes fastest.
Arguments:
- tokens: bfloat16 [4, 4096, 960], P('dp', 'ctx'), may hold values from -6 to 6
- positions: int32 [4, 4096], P('dp', 'ctx'), may hold values from 0 to 4095, as said below
- w_qkv: bfloat16 [960, 1600], P('dp'), may hold values from -0.12909944 to 0.12909944
- w_out: bfloat16 [960, 960], P('dp'), may hold values from -3 to 3
- w_gate: bfloat16 [960, 2560], P('dp'), may hold values from -0.1875 to 0.1875
- w_up: bfloat16 [960, 2560], P('dp'), may hold values from -0.1875 to 0.1875
- w_down: bfloat16 [2560, 960], P('dp'), may hold values from -0.125 to 0.125
- g_attn: bfloat16 [960], P('dp'), may hold values from 0.5 to 1.5
- g_mlp: bfloat16 [960], P('dp'), may hold values from 0.5 to 1.5
- grad_out: bfloat16 [4, 4096, 960], P('dp', 'ctx'), may hold values from -6 to 6
Outputs:
- output: bfloat16 [4, 4096, 960], P('dp', 'ctx')
- grad_tokens: bfloat16 [4, 4096, 960], P('dp', 'ctx')
- grad_qkv: float32 [960, 1600], P('dp')
- grad_wo: float32 [960, 960], P('dp')
- grad_gate: float32 [960, 2560], P('dp')
- grad_up: float32 [960, 2560], P('dp')
- grad_down: float32 [2560, 960], P('dp')
- grad_g_attn: float32 [960], P('dp')
- grad_g_mlp: float32 [960], P('dp')
Inputs may be any that keep to these rules, and one draw needn't show every extreme that they name: In each sequence positions are a permutation of 0 to 4095: stored tokens in rows r * 512 to (r + 1) * 512 - 1 hold two runs of 256 consecutive positions in rising order, position blocks b and 15 - b of 256 positions each, with b differing from r to r.
All inputs are finite; a program needn't handle non-finite values.
Results may differ from a plain program's by a relative error of at most 0.023.
Values may be sent and summed in bfloat16 or wider, within the bound.
No kernel may reach another device: no remote copies, remote signals or barrier semaphores. Data moves between devices by JAX's collectives and lax.ppermute only.
A program may use at most 256 MiB of HBM per device.

v0:
```python
import jax
import jax.numpy as jnp
from jax import lax
from jax.sharding import PartitionSpec as P

QUERY_HEADS = 15
KEY_VALUE_HEADS = 5
HEAD_SIZE = 64


EPS = 1e-05
THETA = 10000.0
MASK_FILL = -1e30


def rope_tables(seq_pos, head_dim):
    half_dim = head_dim // 2
    freqs = THETA ** (-(jnp.arange(half_dim).astype(jnp.float32) * 2.0) / head_dim)
    angles = seq_pos.astype(jnp.float32)[:, None] * freqs[None, :]
    angles = jnp.concatenate([angles, angles], axis=1)
    return (jnp.cos(angles)[:, None, :], jnp.sin(angles)[:, None, :])


def apply_rotation(values, cosine_table, sine_table):
    half_dim = values.shape[-1] // 2
    turned = jnp.concatenate([-values[..., half_dim:], values[..., :half_dim]], axis=-1)
    return values * cosine_table + turned * sine_table


def unrotate(grads, cosine_table, sine_table):
    half_dim = grads.shape[-1] // 2
    moved = grads * sine_table
    turned = jnp.concatenate([moved[..., half_dim:], -moved[..., :half_dim]], axis=-1)
    return grads * cosine_table + turned


def norm_forward(inputs, gain):
    factor = lax.rsqrt(jnp.mean(inputs * inputs, axis=-1, keepdims=True) + EPS)
    return (factor, (inputs * factor * gain.astype(jnp.float32)).astype(jnp.bfloat16))


def norm_backward(inputs, factor, gain, grad_normed):
    scaled = grad_normed * gain.astype(jnp.float32)
    grad_inputs = factor * scaled - inputs * factor**3 * jnp.mean(
        scaled * inputs, axis=-1, keepdims=True
    )
    grad_gain = jnp.sum(grad_normed * inputs * factor, axis=0)
    return (grad_inputs, grad_gain)


def split_pairs(stacked, kv_heads, head_dim):
    key_value_width = kv_heads * head_dim
    key_part = stacked[:, :key_value_width].reshape(stacked.shape[0], kv_heads, head_dim)
    value_part = stacked[:, key_value_width:].reshape(stacked.shape[0], kv_heads, head_dim)
    return (key_part, value_part)


def block_scores(query_rows, key_part, query_pos, key_pos, scaling):
    products = (
        jnp.einsum("bkgh,nkh->kgbn", query_rows, key_part, preferred_element_type=jnp.float32)
        * scaling
    )
    allowed = key_pos[None, :] <= query_pos[:, None]
    return jnp.where(allowed[None, None], products, MASK_FILL)


def forward_fold(query_rows, query_pos, scaling, key_rows):
    kv_heads = query_rows.shape[1]
    head_dim = query_rows.shape[3]

    def forward_step(running, key_item):
        row_max, row_sum, weighted = running
        key_block, key_pos = key_item
        key_part, value_part = split_pairs(key_block, kv_heads, head_dim)
        scores = block_scores(query_rows, key_part, query_pos, key_pos, scaling)
        new_max = jnp.maximum(row_max, jnp.max(scores, axis=-1))
        shrink = jnp.exp(row_max - new_max)
        exps = jnp.exp(scores - new_max[..., None])
        row_sum = row_sum * shrink + jnp.sum(exps, axis=-1)
        weighted = weighted * shrink[..., None] + jnp.einsum(
            "kgbn,nkh->kgbh", exps, value_part.astype(jnp.float32)
        )
        return ((new_max, row_sum, weighted), None)

    def fold(running, gathered, offset):
        key_block, key_pos = gathered
        block_count = key_block.shape[0] // key_rows
        items = (
            key_block.reshape(block_count, key_rows, key_block.shape[1]),
            key_pos.reshape(block_count, key_rows),
        )
        running, _ = lax.scan(forward_step, running, items)
        return running

    return fold


def backward_fold(query_rows, query_pos, head_gradients, delta, log_sum, scaling, key_rows):
    kv_heads = query_rows.shape[1]
    head_dim = query_rows.shape[3]

    def backward_step(state, key_item):
        grad_query, grad_kv, offset = state
        key_block, key_pos = key_item
        key_part, value_part = split_pairs(key_block, kv_heads, head_dim)
        scores = block_scores(query_rows, key_part, query_pos, key_pos, scaling)
        probs = jnp.exp(scores - log_sum[..., None])
        grad_probs = jnp.einsum(
            "bkgh,nkh->kgbn", head_gradients, value_part, preferred_element_type=jnp.float32
        )
        grad_scores = (probs * (grad_probs - delta[..., None])).astype(jnp.bfloat16)
        grad_query = (
            grad_query
            + jnp.einsum(
                "kgbn,nkh->bkgh", grad_scores, key_part, preferred_element_type=jnp.float32
            )
            * scaling
        )
        grad_key = (
            jnp.einsum(
                "kgbn,bkgh->nkh", grad_scores, query_rows, preferred_element_type=jnp.float32
            )
            * scaling
        )
        grad_value = jnp.einsum(
            "kgbn,bkgh->nkh",
            probs.astype(jnp.bfloat16),
            head_gradients,
            preferred_element_type=jnp.float32,
        )
        rows_here = key_block.shape[0]
        update = jnp.concatenate(
            [grad_key.reshape(rows_here, -1), grad_value.reshape(rows_here, -1)], axis=1
        )
        current = lax.dynamic_slice_in_dim(grad_kv, offset, rows_here, 0)
        grad_kv = lax.dynamic_update_slice_in_dim(grad_kv, current + update, offset, 0)
        return ((grad_query, grad_kv, offset + rows_here), None)

    def fold(state, gathered, offset):
        grad_query, grad_kv = state
        key_block, key_pos = gathered
        block_count = key_block.shape[0] // key_rows
        items = (
            key_block.reshape(block_count, key_rows, key_block.shape[1]),
            key_pos.reshape(block_count, key_rows),
        )
        start_row = jnp.asarray(offset)
        (grad_query, grad_kv, _), _ = lax.scan(
            backward_step, (grad_query, grad_kv, start_row), items
        )
        return (grad_query, grad_kv)

    return fold


def local(tokens, positions, w_qkv, w_out, w_gate, w_up, w_down, g_attn, g_mlp, grad_out):
    full_qkv, full_out, full_gate, full_up, full_down, gain_attn, gain_mlp = (
        lax.all_gather(w_qkv, "dp", axis=0, tiled=True),
        lax.all_gather(w_out, "dp", axis=0, tiled=True),
        lax.all_gather(w_gate, "dp", axis=0, tiled=True),
        lax.all_gather(w_up, "dp", axis=0, tiled=True),
        lax.all_gather(w_down, "dp", axis=0, tiled=True),
        lax.all_gather(g_attn, "dp", axis=0, tiled=True),
        lax.all_gather(g_mlp, "dp", axis=0, tiled=True),
    )
    shard_rows = tokens.shape[1]
    query_groups = QUERY_HEADS // KEY_VALUE_HEADS
    query_width = QUERY_HEADS * HEAD_SIZE
    key_value_width = KEY_VALUE_HEADS * HEAD_SIZE
    scaling = HEAD_SIZE ** (-0.5)
    seq_pos = positions[0]
    resid_in = tokens[0].astype(jnp.float32)
    factor_one, normed_one = norm_forward(resid_in, gain_attn)
    projection_result = jnp.dot(normed_one, full_qkv, preferred_element_type=jnp.float32)
    cosine_table, sine_table = rope_tables(seq_pos, HEAD_SIZE)
    query_rows = apply_rotation(
        projection_result[:, :query_width].reshape(shard_rows, QUERY_HEADS, HEAD_SIZE),
        cosine_table,
        sine_table,
    ).astype(jnp.bfloat16)
    query_rows = query_rows.reshape(shard_rows, KEY_VALUE_HEADS, query_groups, HEAD_SIZE)
    key_part = apply_rotation(
        projection_result[:, query_width : query_width + key_value_width].reshape(
            shard_rows, KEY_VALUE_HEADS, HEAD_SIZE
        ),
        cosine_table,
        sine_table,
    ).astype(jnp.bfloat16)
    value_part = projection_result[:, query_width + key_value_width :].astype(jnp.bfloat16)
    key_vals = jnp.concatenate([key_part.reshape(shard_rows, key_value_width), value_part], axis=1)
    start_state = (
        jnp.full((KEY_VALUE_HEADS, query_groups, shard_rows), MASK_FILL, jnp.float32),
        jnp.zeros((KEY_VALUE_HEADS, query_groups, shard_rows), jnp.float32),
        jnp.zeros((KEY_VALUE_HEADS, query_groups, shard_rows, HEAD_SIZE), jnp.float32),
    )
    fold_forward = forward_fold(query_rows, seq_pos, scaling, shard_rows)
    running = fold_forward(
        start_state,
        (
            lax.all_gather(key_vals, "ctx", axis=0, tiled=True),
            lax.all_gather(seq_pos, "ctx", axis=0, tiled=True),
        ),
        jnp.int32(0),
    )
    row_max, row_sum, weighted = running
    log_sum = row_max + jnp.log(row_sum)
    attention_result = (
        jnp.transpose(weighted / row_sum[..., None], (2, 0, 1, 3))
        .reshape(shard_rows, query_width)
        .astype(jnp.bfloat16)
    )
    resid_mid = resid_in + jnp.dot(attention_result, full_out, preferred_element_type=jnp.float32)
    factor_two, normed_two = norm_forward(resid_mid, gain_mlp)
    gate_pre = jnp.dot(normed_two, full_gate, preferred_element_type=jnp.float32)
    upward = jnp.dot(normed_two, full_up, preferred_element_type=jnp.float32)
    sigmoid_gate = jax.nn.sigmoid(gate_pre)
    activated = (gate_pre * sigmoid_gate * upward).astype(jnp.bfloat16)
    output = (resid_mid + jnp.dot(activated, full_down, preferred_element_type=jnp.float32)).astype(
        jnp.bfloat16
    )
    back_qkv, back_out, back_gate, back_up, back_down, back_gain_attn, back_gain_mlp = (
        full_qkv,
        full_out,
        full_gate,
        full_up,
        full_down,
        gain_attn,
        gain_mlp,
    )
    grad_top = grad_out[0]
    grad_act = jnp.einsum("td,fd->tf", grad_top, back_down, preferred_element_type=jnp.float32)
    grad_gate_rows = (
        grad_act * upward * sigmoid_gate * (1.0 + gate_pre * (1.0 - sigmoid_gate))
    ).astype(jnp.bfloat16)
    grad_up_rows = (grad_act * gate_pre * sigmoid_gate).astype(jnp.bfloat16)
    grad_normed_two = jnp.einsum(
        "tf,df->td", grad_gate_rows, back_gate, preferred_element_type=jnp.float32
    ) + jnp.einsum("tf,df->td", grad_up_rows, back_up, preferred_element_type=jnp.float32)
    grad_mid, grad_gain_mlp = norm_backward(resid_mid, factor_two, back_gain_mlp, grad_normed_two)
    grad_mid = grad_mid + grad_top.astype(jnp.float32)
    grad_mid_half = grad_mid.astype(jnp.bfloat16)
    head_gradients = jnp.einsum(
        "td,cd->tc", grad_mid_half, back_out, preferred_element_type=jnp.float32
    ).astype(jnp.bfloat16)
    head_gradients = head_gradients.reshape(shard_rows, KEY_VALUE_HEADS, query_groups, HEAD_SIZE)
    delta = jnp.einsum(
        "bkgh,bkgh->kgb",
        head_gradients,
        attention_result.reshape(shard_rows, KEY_VALUE_HEADS, query_groups, HEAD_SIZE),
        preferred_element_type=jnp.float32,
    )
    back_state = (
        jnp.zeros((shard_rows, KEY_VALUE_HEADS, query_groups, HEAD_SIZE), jnp.float32),
        jnp.zeros((shard_rows * lax.axis_size("ctx"), 2 * key_value_width), jnp.float32),
    )
    fold_back = backward_fold(
        query_rows, seq_pos, head_gradients, delta, log_sum, scaling, shard_rows
    )
    grad_query, grad_kv = fold_back(
        back_state,
        (
            lax.all_gather(key_vals, "ctx", axis=0, tiled=True),
            lax.all_gather(seq_pos, "ctx", axis=0, tiled=True),
        ),
        jnp.int32(0),
    )
    local_key_value_gradient = lax.psum_scatter(
        grad_kv.astype(jnp.bfloat16), "ctx", scatter_dimension=0, tiled=True
    ).astype(jnp.float32)
    grad_q_rows = unrotate(
        grad_query.reshape(shard_rows, QUERY_HEADS, HEAD_SIZE), cosine_table, sine_table
    ).reshape(shard_rows, query_width)
    grad_k_rows = unrotate(
        local_key_value_gradient[:, :key_value_width].reshape(
            shard_rows, KEY_VALUE_HEADS, HEAD_SIZE
        ),
        cosine_table,
        sine_table,
    ).reshape(shard_rows, key_value_width)
    grad_proj = jnp.concatenate(
        [grad_q_rows, grad_k_rows, local_key_value_gradient[:, key_value_width:]], axis=1
    ).astype(jnp.bfloat16)
    grad_normed_one = jnp.einsum(
        "tc,dc->td", grad_proj, back_qkv, preferred_element_type=jnp.float32
    )
    grad_in, grad_gain_attn = norm_backward(resid_in, factor_one, back_gain_attn, grad_normed_one)
    grad_in = (grad_in + grad_mid).astype(jnp.bfloat16)
    term_qkv = jnp.einsum("td,tc->dc", normed_one, grad_proj, preferred_element_type=jnp.float32)
    term_out = jnp.einsum(
        "tc,td->cd", attention_result, grad_mid_half, preferred_element_type=jnp.float32
    )
    term_gate = jnp.einsum(
        "td,tf->df", normed_two, grad_gate_rows, preferred_element_type=jnp.float32
    )
    term_up = jnp.einsum("td,tf->df", normed_two, grad_up_rows, preferred_element_type=jnp.float32)
    term_down = jnp.einsum("tf,td->fd", activated, grad_top, preferred_element_type=jnp.float32)
    share_qkv, share_out, share_gate, share_up, share_down, share_attn, share_mlp = (
        lax.psum_scatter(
            term_qkv.astype(jnp.bfloat16), "dp", scatter_dimension=0, tiled=True
        ).astype(jnp.float32),
        lax.psum_scatter(
            term_out.astype(jnp.bfloat16), "dp", scatter_dimension=0, tiled=True
        ).astype(jnp.float32),
        lax.psum_scatter(
            term_gate.astype(jnp.bfloat16), "dp", scatter_dimension=0, tiled=True
        ).astype(jnp.float32),
        lax.psum_scatter(
            term_up.astype(jnp.bfloat16), "dp", scatter_dimension=0, tiled=True
        ).astype(jnp.float32),
        lax.psum_scatter(
            term_down.astype(jnp.bfloat16), "dp", scatter_dimension=0, tiled=True
        ).astype(jnp.float32),
        lax.psum_scatter(
            grad_gain_attn.astype(jnp.bfloat16), "dp", scatter_dimension=0, tiled=True
        ).astype(jnp.float32),
        lax.psum_scatter(
            grad_gain_mlp.astype(jnp.bfloat16), "dp", scatter_dimension=0, tiled=True
        ).astype(jnp.float32),
    )
    total_qkv, total_out, total_gate, total_up, total_down, total_attn, total_mlp = (
        lax.psum(share_qkv.astype(jnp.bfloat16), "ctx").astype(jnp.float32),
        lax.psum(share_out.astype(jnp.bfloat16), "ctx").astype(jnp.float32),
        lax.psum(share_gate.astype(jnp.bfloat16), "ctx").astype(jnp.float32),
        lax.psum(share_up.astype(jnp.bfloat16), "ctx").astype(jnp.float32),
        lax.psum(share_down.astype(jnp.bfloat16), "ctx").astype(jnp.float32),
        lax.psum(share_attn.astype(jnp.bfloat16), "ctx").astype(jnp.float32),
        lax.psum(share_mlp.astype(jnp.bfloat16), "ctx").astype(jnp.float32),
    )
    return (
        output[None],
        grad_in[None],
        total_qkv,
        total_out,
        total_gate,
        total_up,
        total_down,
        total_attn,
        total_mlp,
    )


def solution(mesh):
    placed = (
        P("dp", "ctx", None),
        P("dp", "ctx"),
        P("dp", None),
        P("dp", None),
        P("dp", None),
        P("dp", None),
        P("dp", None),
        P("dp"),
        P("dp"),
        P("dp", "ctx", None),
    )
    return jax.shard_map(
        local,
        mesh=mesh,
        in_specs=placed,
        out_specs=(
            P("dp", "ctx", None),
            P("dp", "ctx", None),
            P("dp", None),
            P("dp", None),
            P("dp", None),
            P("dp", None),
            P("dp", None),
            P("dp"),
            P("dp"),
        ),
        check_vma=False,
    )
```

profile of v0, /device:TPU:0, one launch (start us, length us, event | category | flops | bytes accessed | tf_op | source)
XLA Modules:
  0.0 1161.0 jit_solution(11415305215108664101)
XLA Ops:
  12.4 11.4 all-reduce.8
  26.3 30.6 %all-gather.8.cloned.1.call-done = bf16[960,1600]{1,0:T(8,128)(2,1)} async-done(((bf16[240,1600]{1,0:T(8,128)(2,1)}), bf16[960,1600]{1,0:T(8,128)(2,1)}) %all-gather.8.cloned.1.call-update) | async-done | bytes 3072016 | tf_op jit(solution)/shard_map/all_gather | solution.py:158
  66.4 13.1 %all-gather = s32[1,4096]{1,0:T(1,128)S(1)} all-gather(s32[1,512]{1,0:T(1,128)S(1)} %copy-done.27), channel_id=2, replica_groups=mesh['dp'=4,'ctx'=8] {'ctx'}, dimensions={1}, use_global_device_ids=true | all-gather | bytes 18432 | tf_op jit(solution)/shard_map/all_gather | solution.py:201
  83.4 36.7 %all-gather.10.cloned.1.call-done = bf16[4096,640]{0,1:T(8,128)(2,1)} async-done(((bf16[512,640]{0,1:T(8,128)(2,1)}), bf16[4096,640]{0,1:T(8,128)(2,1)}) %all-gather.10.cloned.1.call-update) | async-done | bytes 5242896 | tf_op jit(solution)/shard_map/all_gather | solution.py:200
  125.4 233.6 %while.31 = (s32[]{:T(128)}, f32[5,3,512]{2,1,0:T(4,128)S(1)}, f32[5,3,512]{2,1,0:T(4,128)S(1)}, f32[5,3,512,64]{2,3,1,0:T(8,128)}, s32[8,512]{1,0:T(8,128)S(1)}...) while((s32[]{:T(128)}, f32[5,3,512]{2,1,0:T(4,128)S(1)}, ...), condition=%wide.region_4.5_spmd.clone, body=%wide.region_1.4_spmd.clone.sunk | while | flops 1047729664 | bytes 56926332 | solution.py:92
  134.3 8.7 fusion.128
  143.0 10.4 fusion.130
  162.4 9.8 fusion.128
  172.2 11.1 fusion.130
  192.3 8.7 fusion.128
  201.0 11.1 fusion.130
  221.0 9.9 fusion.128
  230.9 11.1 fusion.130
  251.4 8.7 fusion.128
  260.1 11.1 fusion.130
  280.1 9.4 fusion.128
  289.6 11.1 fusion.130
  310.0 8.7 fusion.128
  318.7 11.1 fusion.130
  338.8 8.7 fusion.128
  347.5 11.1 fusion.130
  383.5 10.7 multiply_convert_fusion
  412.8 278.5 %while.32 = (s32[]{:T(128)}, f32[512,5,3,64]{0,3,2,1:T(8,128)S(1)}, f32[4096,640]{0,1:T(8,128)}, bf16[8,512,640]{1,2,0:T(8,128)(2,1)}, s32[8,512]{1,0:T(8,128)S(...) while((s32[]{:T(128)}, f32[512,5,3,64]{0,3,2,1:T(8,128)S(1)}, ...), condition=%wide.region_8.9_spmd.clone, body=%wide.region_7.8_spmd.clone.sunk | while | flops 2558459904 | bytes 90999016 | solution.py:148
  422.2 10.2 fusion.144
  432.4 8.5 fusion.143
  456.9 10.2 fusion.144
  467.2 8.5 fusion.143
  491.7 10.2 fusion.144
  502.0 8.5 fusion.143
  526.6 10.2 fusion.144
  536.8 8.5 fusion.143
  561.3 10.2 fusion.144
  571.6 8.5 fusion.143
  596.1 10.2 fusion.144
  606.3 8.5 fusion.143
  630.9 10.2 fusion.144
  641.1 8.5 fusion.143
  665.7 10.2 fusion.144
  675.9 8.5 fusion.143
  734.7 22.7 %reduce-scatter.11.cloned.1.call-done = bf16[512,640]{0,1:T(8,128)(2,1)} async-done(((bf16[4096,640]{0,1:T(8,128)(2,1)}), bf16[512,640]{0,1:T(8,128)(2,1)}) %reduce-scatter.11.cloned.1.call-update) | async-done | bytes 655376 | tf_op jit(solution)/shard_map/reduce_scatter | solution.py:267
  764.0 56.2 %reduce-scatter.19.cloned.1.call-done = bf16[640,960]{1,0:T(8,128)(2,1)} async-done(((bf16[2560,960]{1,0:T(8,128)(2,1)}), bf16[640,960]{1,0:T(8,128)(2,1)}) %reduce-scatter.19.cloned.1.call-update) | async-done | bytes 1228816
  822.6 35.4 %reduce-scatter.13.cloned.1.call-done = bf16[240,960]{1,0:T(8,128)(2,1)} async-done(((bf16[960,960]{1,0:T(8,128)(2,1)}), bf16[240,960]{1,0:T(8,128)(2,1)}) %reduce-scatter.13.cloned.1.call-update) | async-done | bytes 460816 | tf_op jit(solution)/shard_map/reduce_scatter | solution.py:301
  857.9 61.7 %reduce-scatter.17.cloned.1.call-done = bf16[240,2560]{1,0:T(8,128)(2,1)} async-done(((bf16[960,2560]{1,0:T(8,128)(2,1)}), bf16[240,2560]{1,0:T(8,128)(2,1)}) %reduce-scatter.17.cloned.1.call-update) | async-done | bytes 1228816 | tf_op jit(solution)/shard_map/reduce_scatter | solution.py:307
  919.6 61.8 %reduce-scatter.15.cloned.1.call-done = bf16[240,2560]{1,0:T(8,128)(2,1)} async-done(((bf16[960,2560]{1,0:T(8,128)(2,1)}), bf16[240,2560]{1,0:T(8,128)(2,1)}) %reduce-scatter.15.cloned.1.call-update) | async-done | bytes 1228816 | tf_op jit(solution)/shard_map/reduce_scatter | solution.py:304
  981.4 47.6 %reduce-scatter.21.cloned.1.call-done = bf16[240,1600]{1,0:T(8,128)(2,1)} async-done(((bf16[960,1600]{1,0:T(8,128)(2,1)}), bf16[240,1600]{1,0:T(8,128)(2,1)}) %reduce-scatter.21.cloned.1.call-update) | async-done | bytes 768016
  1041.0 8.9 all-reduce.7
  1050.0 15.5 %all-reduce.5 = (bf16[240]{0:T(256)(128)(2,1)S(1)}, bf16[240]{0:T(256)(128)(2,1)S(1)}) all-reduce(bf16[240]{0:T(256)(128)(2,1)S(1)} %dynamic-slice.5, bf16[240]{0:T(256)(128)(2,1)S(1)} %dynamic-slice.7), channel_id=1, replica_groups=mesh['dp'=4,'ctx'=8] {'ctx'}, use_global_device_ids=true, to_apply=%region_23.24 | all-reduce | flops 480 | bytes 1920 | tf_op jit(solution)/shard_map/psum | solution.py:326
  1069.7 75.9 %all-reduce.11.cloned.1.call-done = (bf16[240,1600]{1,0:T(8,128)(2,1)}, bf16[240,960]{1,0:T(8,128)(2,1)}, bf16[240,2560]{1,0:T(8,128)(2,1)}, bf16[240,2560]{1,0:T(8,128)(2,1)}, bf16[640,960]{0,1:T(8,128)(2,1)}) async-done(((bf16[240,1600]{1,0:T(8,128)(2,1)}, bf16[240,960]{1,0:T(8,128)(2,1)}, bf16[240,2560]{1,0:T(8,128)(2,1)}, bf16[240,2560]{1,0:T(8,128)(2,1)}, bf16[640,960]{0,1:T(8,128)(2,1)}), ...) | async-done | bytes 4915216 | tf_op jit(solution)/shard_map/psum | solution.py:321
  (323 shorter events, 345.0 us)
Async XLA Ops:
  7.2 49.8 %all-gather.8.cloned.1.call-start = ((), (), s32[]{:S(2)}) async-start(), calls=%async_computation.6 | async-start | bytes 3993600 | tf_op jit(solution)/shard_map/all_gather | solution.py:158
  7.9 112.2 %all-gather.10.cloned.1.call-start = ((), (), s32[]{:S(2)}) async-start(), calls=%async_computation.7 | async-start | bytes 5898240 | tf_op jit(solution)/shard_map/all_gather | solution.py:200
  23.8 37.5 %copy-start.28 = (f32[960]{0:T(1024)}, f32[960]{0:T(1024)S(1)}, u32[]{:S(2)}) copy-start(f32[960]{0:T(1024)S(1)} %convert_element_type.156) | copy-start | bytes 11524
  24.2 58.6 %copy-start.11 = (f32[512,64]{0,1:T(8,128)}, f32[512,64]{0,1:T(8,128)S(1)}, u32[]{:S(2)}) copy-start(f32[512,64]{0,1:T(8,128)S(1)} %get-tuple-element.396) | copy-start | bytes 393220
  24.2 58.6 %copy-start.13 = (f32[512,64]{0,1:T(8,128)}, f32[512,64]{0,1:T(8,128)S(1)}, u32[]{:S(2)}) copy-start(f32[512,64]{0,1:T(8,128)S(1)} %get-tuple-element.397) | copy-start | bytes 393220
  26.3 35.0 %copy-start.31 = (f32[512]{0:T(512)}, f32[512]{0:T(512)S(1)}, u32[]{:S(2)}) copy-start(f32[512]{0:T(512)S(1)} %get-tuple-element.399) | copy-start | bytes 6148
  61.3 1.7 copy-start.9
  63.8 2.6 copy-start.27
  63.9 297.9 %all-gather.12.cloned.1.call-start = ((), (), s32[]{:S(2)}) async-start(), calls=%async_computation.8 | async-start | bytes 2457600 | tf_op jit(solution)/shard_map/all_gather | solution.py:159
  64.6 303.0 %all-gather.16.cloned.1.call-start = ((), (), s32[]{:S(2)}) async-start(), calls=%async_computation.10 | async-start | bytes 6144000 | tf_op jit(solution)/shard_map/all_gather | solution.py:161
  65.2 310.3 %all-gather.14.cloned.1.call-start = ((), (), s32[]{:S(2)}) async-start(), calls=%async_computation.9 | async-start | bytes 6144000 | tf_op jit(solution)/shard_map/all_gather | solution.py:160
  65.8 317.7 %all-gather.18.cloned.1.call-start = ((), (), s32[]{:S(2)}) async-start(), calls=%async_computation.11 | async-start | bytes 6144000 | tf_op jit(solution)/shard_map/all_gather | solution.py:162
  66.3 691.0 %reduce-scatter.11.cloned.1.call-start = ((), (), s32[]{:S(2)}) async-start(), calls=%async_computation.12 | async-start | bytes 5898240 | tf_op jit(solution)/shard_map/reduce_scatter | solution.py:267
  383.5 10.7 copy-start.8
  394.1 2.8 copy-start.36
  394.1 2.8 copy-start.37
  394.2 3.0 copy-start.3
  397.2 6.1 copy-start.19
  404.8 2.3 copy-start.5
  443.4 1.6 copy-start
  478.2 1.6 copy-start
  513.0 1.6 copy-start
  547.8 1.6 copy-start
  582.6 1.6 copy-start
  617.4 1.6 copy-start
  652.1 1.6 copy-start
  686.9 1.6 copy-start
  698.4 121.8 %reduce-scatter.19.cloned.1.call-start = ((), (), s32[]{:S(2)}) async-start(), calls=%async_computation.16 | async-start | bytes 6553600
  713.9 4.6 copy-start.1
  713.9 144.0 %reduce-scatter.13.cloned.1.call-start = ((), (), s32[]{:S(2)}) async-start(), calls=%async_computation.13 | async-start | bytes 2457600 | tf_op jit(solution)/shard_map/reduce_scatter | solution.py:301
  718.4 201.2 %reduce-scatter.17.cloned.1.call-start = ((), (), s32[]{:S(2)}) async-start(), calls=%async_computation.15 | async-start | bytes 6144000 | tf_op jit(solution)/shard_map/reduce_scatter | solution.py:307
  724.6 256.7 %reduce-scatter.15.cloned.1.call-start = ((), (), s32[]{:S(2)}) async-start(), calls=%async_computation.14 | async-start | bytes 6144000 | tf_op jit(solution)/shard_map/reduce_scatter | solution.py:304
  730.9 298.1 %reduce-scatter.21.cloned.1.call-start = ((), (), s32[]{:S(2)}) async-start(), calls=%async_computation.17 | async-start | bytes 3993600
  758.6 1.6 copy-start.21
  758.6 1.6 copy-start.29
  758.6 1.6 copy-start.32
  763.9 381.7 %all-reduce.11.cloned.1.call-start = ((), (), s32[]{:S(2)}) async-start(), calls=%async_computation.18 | async-start | bytes 9953280 | tf_op jit(solution)/shard_map/psum | solution.py:321
  1028.9 1.5 copy-start.4
  1030.5 7.0 copy-start.22
  1030.5 7.0 copy-start.26
  1030.5 7.0 copy-start.34
  1037.5 3.4 copy-start.33
  1037.5 29.2 %copy-start.7 = (f32[512,960]{0,1:T(8,128)S(1)}, f32[512,960]{0,1:T(8,128)}, u32[]{:S(2)}) copy-start(f32[512,960]{0,1:T(8,128)} %copy-done.6) | copy-start | bytes 5898244
  1037.5 29.2 %copy-start.30 = (f32[512]{0:T(512)S(1)}, f32[512]{0:T(512)}, u32[]{:S(2)}) copy-start(f32[512]{0:T(512)} %get-tuple-element.398) | copy-start | bytes 6148
  1145.6 2.5 copy-start.24
  1145.6 3.6 copy-start.18
  1148.2 2.8 copy-start.17
  1150.9 1.7 copy-start.16
  (10 other events, 11.9 us)
Sparse Core Ops, SparseCore 0:
  9.9 47.0 all-gather.7
  64.0 56.0 all-gather.9
  121.9 33.0 all-gather.11
  156.7 58.6 all-gather.15
  217.1 58.6 all-gather.13
  277.5 58.6 all-gather.17
  698.5 58.7 reduce-scatter.10
  760.3 59.8 reduce-scatter.18
  823.9 34.0 reduce-scatter.12
  860.8 58.7 reduce-scatter.16
  922.6 58.7 reduce-scatter.14
  984.2 44.6 reduce-scatter.20
  1032.5 113.0 all-reduce.10
where the time goes:
time: 1170 us; the launch traced here: 1160 us
  matrix products  469 us (40%)
  waiting for transfers between devices  432 us (37%)
  other arithmetic  133 us (11%)
  local copies, waits for them, and re-layouts  61 us (5%)
  blocking collectives  49 us (4%)
  between operations  16 us (1%)
    dot_general x16, matrix products, block_scores(): jnp.einsum('bkgh,nkh->kgbn', query_rows, key_part, preferred_element_type...  117 us
    unnamed x15, waiting for transfers between devices  107 us
    dot_general x8, matrix products, forward_step(): jnp.einsum('kgbn,nkh->kgbh', exps, value_part.astype(jnp.float32))  88 us
    dot_general x8, matrix products, backward_step(): jnp.einsum('kgbn,bkgh->nkh', probs.astype(jnp.bfloat16), head_gradients,...  81.9 us
    psum x1, waiting for transfers between devices, local(): lax.psum(share_qkv.astype(jnp.bfloat16), 'ctx').astype(jnp.float32)  75.9 us
    reduce_sum x8, other arithmetic, forward_step(): row_sum = row_sum * shrink + jnp.sum(exps, axis=-1)  72.3 us
    dot_general x8, matrix products, backward_step(): jnp.einsum('bkgh,nkh->kgbn', head_gradients, value_part, preferred_elemen...  68.3 us
    reduce_scatter x1, waiting for transfers between devices, local(): lax.psum_scatter(term_gate.astype(jnp.bfloat16), 'dp', scatter_dimension=...  61.8 us
  transfers between devices with their start and end apart: 13, of which 9 were waited for; matrix products, arithmetic and copies ran while one was open for 28% of the time, Pallas kernels for 0%

commit v1 on v0

--- a/solution.py
+++ b/solution.py
@@ -1,11 +1,16 @@
+import functools
+
 import jax
 import jax.numpy as jnp
 from jax import lax
+from jax.experimental import pallas as pl
+from jax.experimental.pallas import tpu as pltpu
 from jax.sharding import PartitionSpec as P
 
 QUERY_HEADS = 15
 KEY_VALUE_HEADS = 5
 HEAD_SIZE = 64
+GROUPS = QUERY_HEADS // KEY_VALUE_HEADS
 
 
 EPS = 1e-05
@@ -48,111 +53,140 @@
     return (grad_inputs, grad_gain)
 
 
-def split_pairs(stacked, kv_heads, head_dim):
-    key_value_width = kv_heads * head_dim
-    key_part = stacked[:, :key_value_width].reshape(stacked.shape[0], kv_heads, head_dim)
-    value_part = stacked[:, key_value_width:].reshape(stacked.shape[0], kv_heads, head_dim)
-    return (key_part, value_part)
-
-
-def block_scores(query_rows, key_part, query_pos, key_pos, scaling):
-    products = (
-        jnp.einsum("bkgh,nkh->kgbn", query_rows, key_part, preferred_element_type=jnp.float32)
-        * scaling
-    )
-    allowed = key_pos[None, :] <= query_pos[:, None]
-    return jnp.where(allowed[None, None], products, MASK_FILL)
-
-
-def forward_fold(query_rows, query_pos, scaling, key_rows):
-    kv_heads = query_rows.shape[1]
-    head_dim = query_rows.shape[3]
-
-    def forward_step(running, key_item):
-        row_max, row_sum, weighted = running
-        key_block, key_pos = key_item
-        key_part, value_part = split_pairs(key_block, kv_heads, head_dim)
-        scores = block_scores(query_rows, key_part, query_pos, key_pos, scaling)
-        new_max = jnp.maximum(row_max, jnp.max(scores, axis=-1))
-        shrink = jnp.exp(row_max - new_max)
-        exps = jnp.exp(scores - new_max[..., None])
-        row_sum = row_sum * shrink + jnp.sum(exps, axis=-1)
-        weighted = weighted * shrink[..., None] + jnp.einsum(
-            "kgbn,nkh->kgbh", exps, value_part.astype(jnp.float32)
-        )
-        return ((new_max, row_sum, weighted), None)
-
-    def fold(running, gathered, offset):
-        key_block, key_pos = gathered
-        block_count = key_block.shape[0] // key_rows
-        items = (
-            key_block.reshape(block_count, key_rows, key_block.shape[1]),
-            key_pos.reshape(block_count, key_rows),
-        )
-        running, _ = lax.scan(forward_step, running, items)
-        return running
-
-    return fold
-
-
-def backward_fold(query_rows, query_pos, head_gradients, delta, log_sum, scaling, key_rows):
-    kv_heads = query_rows.shape[1]
-    head_dim = query_rows.shape[3]
-
-    def backward_step(state, key_item):
-        grad_query, grad_kv, offset = state
-        key_block, key_pos = key_item
-        key_part, value_part = split_pairs(key_block, kv_heads, head_dim)
-        scores = block_scores(query_rows, key_part, query_pos, key_pos, scaling)
-        probs = jnp.exp(scores - log_sum[..., None])
-        grad_probs = jnp.einsum(
-            "bkgh,nkh->kgbn", head_gradients, value_part, preferred_element_type=jnp.float32
-        )
-        grad_scores = (probs * (grad_probs - delta[..., None])).astype(jnp.bfloat16)
-        grad_query = (
-            grad_query
-            + jnp.einsum(
-                "kgbn,nkh->bkgh", grad_scores, key_part, preferred_element_type=jnp.float32
-            )
-            * scaling
-        )
-        grad_key = (
-            jnp.einsum(
-                "kgbn,bkgh->nkh", grad_scores, query_rows, preferred_element_type=jnp.float32
-            )
-            * scaling
-        )
-        grad_value = jnp.einsum(
-            "kgbn,bkgh->nkh",
-            probs.astype(jnp.bfloat16),
-            head_gradients,
-            preferred_element_type=jnp.float32,
-        )
-        rows_here = key_block.shape[0]
-        update = jnp.concatenate(
-            [grad_key.reshape(rows_here, -1), grad_value.reshape(rows_here, -1)], axis=1
-        )
-        current = lax.dynamic_slice_in_dim(grad_kv, offset, rows_here, 0)
-        grad_kv = lax.dynamic_update_slice_in_dim(grad_kv, current + update, offset, 0)
-        return ((grad_query, grad_kv, offset + rows_here), None)
-
-    def fold(state, gathered, offset):
-        grad_query, grad_kv = state
-        key_block, key_pos = gathered
-        block_count = key_block.shape[0] // key_rows
-        items = (
-            key_block.reshape(block_count, key_rows, key_block.shape[1]),
-            key_pos.reshape(block_count, key_rows),
-        )
-        start_row = jnp.asarray(offset)
-        (grad_query, grad_kv, _), _ = lax.scan(
-            backward_step, (grad_query, grad_kv, start_row), items
-        )
-        return (grad_query, grad_kv)
-
-    return fold
-
-
+def list_pairs(qblk, kblk, lst, nblk):
+    cnt=jnp.int32(0)
+    for r in range(2):
+        def body(j,c,r=r):
+            act=kblk[j]<qblk[r]
+            @pl.when(act)
+            def _():
+                lst[c]=r*256+j
+            return c+act.astype(jnp.int32)
+        cnt=lax.fori_loop(0,nblk,body,cnt)
+    return cnt
+
+def forward_kernel(nblk, run, qblk, kblk, own, qT, kv, oT, lse, m_s, l_s, acc_s, lst):
+    list_pairs(qblk,kblk,lst,nblk)
+    tri=lax.broadcasted_iota(jnp.int32,(run,run),0)<=lax.broadcasted_iota(jnp.int32,(run,run),1)
+    def pair(rank,ko,qo,diag):
+        def sdot(hd):
+            h=hd//GROUPS
+            k=kv[rank,h*HEAD_SIZE:(h+1)*HEAD_SIZE,pl.ds(ko,run)].T
+            q=qT[hd*HEAD_SIZE:(hd+1)*HEAD_SIZE,pl.ds(qo,run)]
+            return jnp.dot(k,q,preferred_element_type=jnp.float32)
+        if not diag:
+            mo_all=m_s[:,pl.ds(qo,run)]
+            lo_all=l_s[:,pl.ds(qo,run)]
+        ms=[];ls=[]
+        nxt=sdot(0)
+        pend=None
+        def flush(pend):
+            hd,p,al=pend
+            h=hd//GROUPS
+            vT=kv[rank,(KEY_VALUE_HEADS+h)*HEAD_SIZE:(KEY_VALUE_HEADS+h+1)*HEAD_SIZE,pl.ds(ko,run)]
+            o=jnp.dot(vT,p,preferred_element_type=jnp.float32)
+            if al is None: acc_s[hd*HEAD_SIZE:(hd+1)*HEAD_SIZE,pl.ds(qo,run)]=o
+            else: acc_s[hd*HEAD_SIZE:(hd+1)*HEAD_SIZE,pl.ds(qo,run)]=acc_s[hd*HEAD_SIZE:(hd+1)*HEAD_SIZE,pl.ds(qo,run)]*al+o
+        def mx(hd,s):
+            if diag: s=jnp.where(tri,s,MASK_FILL)
+            mn=jnp.max(s,axis=0,keepdims=True)
+            if not diag: mn=jnp.maximum(mo_all[hd:hd+1],mn)
+            return s,mn
+        s1=sdot(1)
+        cur=mx(0,nxt)
+        for hd in range(QUERY_HEADS):
+            s,mn=cur
+            if hd+1<QUERY_HEADS:
+                cur=mx(hd+1,s1)
+            if hd+2<QUERY_HEADS: s1=sdot(hd+2)
+            if pend is not None: flush(pend)
+            p=jnp.exp(s-mn)
+            if diag:
+                al=None; l=jnp.sum(p,axis=0,keepdims=True)
+            else:
+                al=jnp.exp(mo_all[hd:hd+1]-mn)
+                l=lo_all[hd:hd+1]*al+jnp.sum(p,axis=0,keepdims=True)
+            ms.append(mn); ls.append(l)
+            pend=(hd,p.astype(jnp.bfloat16),al)
+        flush(pend)
+        m_s[:,pl.ds(qo,run)]=jnp.concatenate(ms+[ms[-1]],0)
+        l_s[:,pl.ds(qo,run)]=jnp.concatenate(ls+[ls[-1]],0)
+    for r in range(2):
+        pair(own[0],r*run,r*run,True)
+    def body(i,_):
+        c=lst[i]
+        r=c//256; j=c%256
+        pair(j//2,pl.multiple_of((j%2)*run,run),pl.multiple_of(r*run,run),False)
+        return 0
+    lax.fori_loop(0,nblk-1,body,0)
+    lse[...]=m_s[...]+jnp.log(l_s[...])
+    for hd in range(QUERY_HEADS):
+        oT[hd*HEAD_SIZE:(hd+1)*HEAD_SIZE,:]=(acc_s[hd*HEAD_SIZE:(hd+1)*HEAD_SIZE,:]/l_s[hd:hd+1,:]).astype(jnp.bfloat16)
+
+def attention_forward(qblk,kblk,own,qT,kv):
+    n=kv.shape[0]; T=qT.shape[1]; run=T//2
+    sm=pl.BlockSpec(memory_space=pltpu.SMEM); vm=pl.BlockSpec(memory_space=pltpu.VMEM)
+    return pl.pallas_call(functools.partial(forward_kernel,2*n,run),
+        out_shape=(jax.ShapeDtypeStruct((QUERY_HEADS*HEAD_SIZE,T),jnp.bfloat16),jax.ShapeDtypeStruct((16,T),jnp.float32)),
+        in_specs=[sm,sm,sm,vm,vm],out_specs=(vm,vm),
+        scratch_shapes=[pltpu.VMEM((16,T),jnp.float32),pltpu.VMEM((16,T),jnp.float32),pltpu.VMEM((QUERY_HEADS*HEAD_SIZE,T),jnp.float32),pltpu.SMEM((4*n,),jnp.int32)],
+        compiler_params=pltpu.CompilerParams(vmem_limit_bytes=60*2**20),name="attn_fwd")(qblk,kblk,own,qT,kv)
+
+def backward_kernel(nblk, run, qblk, kblk, own, qT, kv, oT, lse, doT, dqT, dkv, dq_s, dkv_s, dl_s, lst):
+    list_pairs(qblk,kblk,lst,nblk)
+    tri=lax.broadcasted_iota(jnp.int32,(run,run),0)<=lax.broadcasted_iota(jnp.int32,(run,run),1)
+    dkv_s[...]=jnp.zeros_like(dkv_s)
+    dq_s[...]=jnp.zeros_like(dq_s)
+    for hd in range(QUERY_HEADS):
+        dl_s[hd:hd+1,:]=jnp.sum(oT[hd*HEAD_SIZE:(hd+1)*HEAD_SIZE,:].astype(jnp.float32)*doT[hd*HEAD_SIZE:(hd+1)*HEAD_SIZE,:].astype(jnp.float32),axis=0,keepdims=True)
+    nt=(((1,),(1,)),((),()))
+    def pair(rank,ko,qo,diag):
+        ls_all=lse[:,pl.ds(qo,run)]
+        dl_all=dl_s[:,pl.ds(qo,run)]
+        def first(hd):
+            h=hd//GROUPS
+            k=kv[rank,h*HEAD_SIZE:(h+1)*HEAD_SIZE,pl.ds(ko,run)].T
+            v=kv[rank,(KEY_VALUE_HEADS+h)*HEAD_SIZE:(KEY_VALUE_HEADS+h+1)*HEAD_SIZE,pl.ds(ko,run)].T
+            q=qT[hd*HEAD_SIZE:(hd+1)*HEAD_SIZE,pl.ds(qo,run)]
+            do=doT[hd*HEAD_SIZE:(hd+1)*HEAD_SIZE,pl.ds(qo,run)]
+            return jnp.dot(k,q,preferred_element_type=jnp.float32),jnp.dot(v,do,preferred_element_type=jnp.float32)
+        def last(hd,p,ds):
+            h=hd//GROUPS
+            q=qT[hd*HEAD_SIZE:(hd+1)*HEAD_SIZE,pl.ds(qo,run)]
+            do=doT[hd*HEAD_SIZE:(hd+1)*HEAD_SIZE,pl.ds(qo,run)]
+            kT=kv[rank,h*HEAD_SIZE:(h+1)*HEAD_SIZE,pl.ds(ko,run)]
+            dkv_s[rank,(KEY_VALUE_HEADS+h)*HEAD_SIZE:(KEY_VALUE_HEADS+h+1)*HEAD_SIZE,pl.ds(ko,run)]+=lax.dot_general(do,p,nt,preferred_element_type=jnp.float32)
+            dkv_s[rank,h*HEAD_SIZE:(h+1)*HEAD_SIZE,pl.ds(ko,run)]+=lax.dot_general(q,ds,nt,preferred_element_type=jnp.float32)
+            dq_s[hd*HEAD_SIZE:(hd+1)*HEAD_SIZE,pl.ds(qo,run)]+=jnp.dot(kT,ds,preferred_element_type=jnp.float32)
+        nxt=first(0); pend=None
+        for hd in range(QUERY_HEADS):
+            s,dp=nxt
+            if hd+1<QUERY_HEADS: nxt=first(hd+1)
+            if pend is not None: last(*pend)
+            p=jnp.exp(s-ls_all[hd:hd+1])
+            if diag: p=jnp.where(tri,p,0.0)
+            ds=(p*(dp-dl_all[hd:hd+1])).astype(jnp.bfloat16)
+            pend=(hd,p.astype(jnp.bfloat16),ds)
+        last(*pend)
+    for r in range(2):
+        pair(own[0],r*run,r*run,True)
+    def body(i,_):
+        c=lst[i]
+        r=c//256; j=c%256
+        pair(j//2,pl.multiple_of((j%2)*run,run),pl.multiple_of(r*run,run),False)
+        return 0
+    lax.fori_loop(0,nblk-1,body,0)
+    dqT[...]=dq_s[...]*(HEAD_SIZE**-0.5)
+    dkv[...]=dkv_s[...].astype(jnp.bfloat16)
+
+def attention_backward(qblk,kblk,own,qT,kv,oT,lse,doT):
+    n=kv.shape[0]; T=qT.shape[1]; run=T//2
+    sm=pl.BlockSpec(memory_space=pltpu.SMEM); vm=pl.BlockSpec(memory_space=pltpu.VMEM)
+    return pl.pallas_call(functools.partial(backward_kernel,2*n,run),
+        out_shape=(jax.ShapeDtypeStruct((QUERY_HEADS*HEAD_SIZE,T),jnp.float32),jax.ShapeDtypeStruct(kv.shape,jnp.bfloat16)),
+        in_specs=[sm,sm,sm,vm,vm,vm,vm,vm],out_specs=(vm,vm),
+        scratch_shapes=[pltpu.VMEM((QUERY_HEADS*HEAD_SIZE,T),jnp.float32),pltpu.VMEM(kv.shape,jnp.float32),pltpu.VMEM((16,T),jnp.float32),pltpu.SMEM((4*n,),jnp.int32)],
+        compiler_params=pltpu.CompilerParams(vmem_limit_bytes=60*2**20),name="attn_bwd")(qblk,kblk,own,qT,kv,oT,lse,doT)
 def local(tokens, positions, w_qkv, w_out, w_gate, w_up, w_down, g_attn, g_mlp, grad_out):
     full_qkv, full_out, full_gate, full_up, full_down, gain_attn, gain_mlp = (
         lax.all_gather(w_qkv, "dp", axis=0, tiled=True),
@@ -178,7 +212,7 @@
         cosine_table,
         sine_table,
     ).astype(jnp.bfloat16)
-    query_rows = query_rows.reshape(shard_rows, KEY_VALUE_HEADS, query_groups, HEAD_SIZE)
+    query_t = (query_rows.reshape(shard_rows, query_width) * jnp.bfloat16(scaling)).T
     key_part = apply_rotation(
         projection_result[:, query_width : query_width + key_value_width].reshape(
             shard_rows, KEY_VALUE_HEADS, HEAD_SIZE
@@ -188,27 +222,13 @@
     ).astype(jnp.bfloat16)
     value_part = projection_result[:, query_width + key_value_width :].astype(jnp.bfloat16)
     key_vals = jnp.concatenate([key_part.reshape(shard_rows, key_value_width), value_part], axis=1)
-    start_state = (
-        jnp.full((KEY_VALUE_HEADS, query_groups, shard_rows), MASK_FILL, jnp.float32),
-        jnp.zeros((KEY_VALUE_HEADS, query_groups, shard_rows), jnp.float32),
-        jnp.zeros((KEY_VALUE_HEADS, query_groups, shard_rows, HEAD_SIZE), jnp.float32),
-    )
-    fold_forward = forward_fold(query_rows, seq_pos, scaling, shard_rows)
-    running = fold_forward(
-        start_state,
-        (
-            lax.all_gather(key_vals, "ctx", axis=0, tiled=True),
-            lax.all_gather(seq_pos, "ctx", axis=0, tiled=True),
-        ),
-        jnp.int32(0),
-    )
-    row_max, row_sum, weighted = running
-    log_sum = row_max + jnp.log(row_sum)
-    attention_result = (
-        jnp.transpose(weighted / row_sum[..., None], (2, 0, 1, 3))
-        .reshape(shard_rows, query_width)
-        .astype(jnp.bfloat16)
-    )
+    run = shard_rows // 2
+    all_kv = lax.all_gather(key_vals.T, "ctx", axis=0)
+    query_blocks = seq_pos[::run] // run
+    key_blocks = lax.all_gather(query_blocks, "ctx", axis=0, tiled=True)
+    own = lax.axis_index("ctx").astype(jnp.int32)[None]
+    attention_t, log_sum = attention_forward(query_blocks, key_blocks, own, query_t, all_kv)
+    attention_result = attention_t.T
     resid_mid = resid_in + jnp.dot(attention_result, full_out, preferred_element_type=jnp.float32)
     factor_two, normed_two = norm_forward(resid_mid, gain_mlp)
     gate_pre = jnp.dot(normed_two, full_gate, preferred_element_type=jnp.float32)
@@ -242,31 +262,13 @@
     head_gradients = jnp.einsum(
         "td,cd->tc", grad_mid_half, back_out, preferred_element_type=jnp.float32
     ).astype(jnp.bfloat16)
-    head_gradients = head_gradients.reshape(shard_rows, KEY_VALUE_HEADS, query_groups, HEAD_SIZE)
-    delta = jnp.einsum(
-        "bkgh,bkgh->kgb",
-        head_gradients,
-        attention_result.reshape(shard_rows, KEY_VALUE_HEADS, query_groups, HEAD_SIZE),
-        preferred_element_type=jnp.float32,
-    )
-    back_state = (
-        jnp.zeros((shard_rows, KEY_VALUE_HEADS, query_groups, HEAD_SIZE), jnp.float32),
-        jnp.zeros((shard_rows * lax.axis_size("ctx"), 2 * key_value_width), jnp.float32),
-    )
-    fold_back = backward_fold(
-        query_rows, seq_pos, head_gradients, delta, log_sum, scaling, shard_rows
-    )
-    grad_query, grad_kv = fold_back(
-        back_state,
-        (
-            lax.all_gather(key_vals, "ctx", axis=0, tiled=True),
-            lax.all_gather(seq_pos, "ctx", axis=0, tiled=True),
-        ),
-        jnp.int32(0),
-    )
+    grad_query_t, grad_kv = attention_backward(
+        query_blocks, key_blocks, own, query_t, all_kv, attention_t, log_sum, head_gradients.T
+    )
+    grad_query = grad_query_t.T
     local_key_value_gradient = lax.psum_scatter(
-        grad_kv.astype(jnp.bfloat16), "ctx", scatter_dimension=0, tiled=True
-    ).astype(jnp.float32)
+        grad_kv, "ctx", scatter_dimension=0, tiled=False
+    ).astype(jnp.float32).T
     grad_q_rows = unrotate(
         grad_query.reshape(shard_rows, QUERY_HEADS, HEAD_SIZE), cosine_table, sine_table
     ).reshape(shard_rows, query_width)

time: 1170 us -> 868 us (0.74)
  matrix products: 469 us -> 81 us
  waiting for transfers between devices: 432 us -> 600 us
  other arithmetic: 133 us -> 26.2 us
  Pallas kernels: 0 us -> 71.6 us
  local copies, waits for them, and re-layouts: 61 us -> 19.9 us
    dot_general x56 -> x0, matrix products: 388 us -> none  [the longest x16 117 us: block_scores(): jnp.einsum('bkgh,nkh->kgbn', query_rows, key_part, preferred_element_type...]
    reduce_sum x8 -> x0, other arithmetic: 72.3 us -> none  [forward_step(): row_sum = row_sum * shrink + jnp.sum(exps, axis=-1)]
    pallas_call x0 -> x2, Pallas kernels: none -> 71.6 us  [the longest x1 40.8 us: attention_backward(): pl.pallas_call(functools.partial(backward_kernel, 2 * n, run), out_shape=...]
    all_gather x1, waiting for transfers between devices: 0.01 us -> 57.1 us  [local(): lax.all_gather(w_up, 'dp', axis=0, tiled=True)]
    all_gather x1, waiting for transfers between devices: 0.01 us -> 53.4 us  [local(): lax.all_gather(w_gate, 'dp', axis=0, tiled=True)]
    all_gather x1, waiting for transfers between devices: 0.01 us -> 53.4 us  [local(): lax.all_gather(w_down, 'dp', axis=0, tiled=True)]
    dynamic_update_slice x8 -> x0, other arithmetic: 21.8 us -> none  [backward_step(): lax.dynamic_update_slice_in_dim(grad_kv, current + update, offset, 0)]
    squeeze x16 -> x0, local copies, waits for them, and re-layouts: 18.2 us -> none  [fold(): running, _ = lax.scan(forward_step, running, items)]
  transfers between devices with their start and end apart: 13 -> 13, of which waited for: 9 -> 13; matrix products, arithmetic and copies ran while one was open for 28% -> 10% of each run, Pallas kernels for 0% -> 4%
where the time goes in v1:
time: 868 us; the launch traced here: 863 us
  waiting for transfers between devices  600 us (69%)
  matrix products  81 us (9%)
  Pallas kernels  71.6 us (8%)
  blocking collectives  47.6 us (5%)
  other arithmetic  26.2 us (3%)
  local copies, waits for them, and re-layouts  19.9 us (2%)
  between operations  16.6 us (2%)
    unnamed x15, waiting for transfers between devices  107 us
    psum x1, waiting for transfers between devices, local(): lax.psum(share_qkv.astype(jnp.bfloat16), 'ctx').astype(jnp.float32)  76.8 us
    reduce_scatter x1, waiting for transfers between devices, local(): lax.psum_scatter(term_gate.astype(jnp.bfloat16), 'dp', scatter_dimension=...  61.8 us
    reduce_scatter x1, waiting for transfers between devices, local(): lax.psum_scatter(term_up.astype(jnp.bfloat16), 'dp', scatter_dimension=0,...  61.6 us
    all_gather x1, waiting for transfers between devices, local(): lax.all_gather(w_up, 'dp', axis=0, tiled=True)  57.1 us
    all_gather x1, waiting for transfers between devices, local(): lax.all_gather(w_gate, 'dp', axis=0, tiled=True)  53.4 us
    all_gather x1, waiting for transfers between devices, local(): lax.all_gather(w_down, 'dp', axis=0, tiled=True)  53.4 us
    pallas_call x1, Pallas kernels, attention_backward(): pl.pallas_call(functools.partial(backward_kernel, 2 * n, run), out_shape=...  40.8 us
  transfers between devices with their start and end apart: 13, of which 13 were waited for; matrix products, arithmetic and copies ran while one was open for 10% of the time, Pallas kernels for 4%

profile of v1, /device:TPU:0, one launch (start us, length us, event | category | flops | bytes accessed | tf_op | source)
XLA Modules:
  0.0 863.3 jit_solution(231746059240882956)
XLA Ops:
  8.7 1.3 fusion.38
  12.3 12.0 %all-reduce.9 = (bf16[960]{0:T(1024)(128)(2,1)S(1)}, bf16[960]{0:T(1024)(128)(2,1)}) all-reduce(bf16[960]{0:T(1024)(128)(2,1)S(1)} %dynamic-update-slice.1, bf16[960]{0:T(1024)(128)(2,1)S(1)} %dynamic-update-slice.2), channel_id=1, replica_groups=mesh['dp'=4,'ctx'=8] {'dp'}, use_global_device_ids=true, to_apply=%add.1 | all-reduce | flops 1920 | bytes 7680
  24.7 1.5 fusion.4
  26.2 30.8 %all-gather.8.cloned.1.call-done = bf16[960,1600]{1,0:T(8,128)(2,1)} async-done(((bf16[240,1600]{1,0:T(8,128)(2,1)}), bf16[960,1600]{1,0:T(8,128)(2,1)}) %all-gather.8.cloned.1.call-update) | async-done | bytes 3072016 | tf_op jit(solution)/shard_map/all_gather | solution.py:192
  57.0 4.3 fusion.29
  65.1 1.3 slice.47
  70.1 11.1 %all-reduce.kblk = s32[16]{0:T(128)} all-reduce(s32[16]{0:T(128)} %get-tuple-element.32), channel_id=1, replica_groups=mesh['dp'=4,'ctx'=8] {'ctx'}, use_global_device_ids=true, to_apply=%add | all-reduce | flops 16 | bytes 128
  81.9 1.5 fusion.17
  83.4 35.5 %all-gather.18.cloned.1.call-done = bf16[5120,512]{1,0:T(8,128)(2,1)} async-done(((bf16[640,512]{1,0:T(8,128)(2,1)}), bf16[5120,512]{1,0:T(8,128)(2,1)}) %all-gather.18.cloned.1.call-update) | async-done | bytes 5242896 | tf_op jit(solution)/shard_map/all_gather | solution.py:226
  118.9 30.8 %attn_fwd.1 = (bf16[960,512]{1,0:T(8,128)(2,1)}, f32[16,512]{1,0:T(8,128)}) custom-call(s32[2]{0:T(128)} %get-tuple-element.33.qblk, s32[16]{0:T(128)} %all-reduce.kblk, s32[1]{0:T(128)} %bitcast.3.own, bf16[960,512]{1,0:T(8,128)(2,1)} %bitcast.102, bf16[8,640,512]{2,1,0:T(8,128)(2,1)} %bitcast.100), custom_call_target="tpu_custom_call" | custom-call | tf_op jit(solution)/shard_map/attn_fwd/pallas_call | solution.py:129
  149.7 4.2 all-gather.10.cloned.1.call-done
  153.9 3.1 multiply_reduce_fusion.2
  157.2 57.1 %all-gather.14.cloned.1.call-done = bf16[960,2560]{1,0:T(8,128)(2,1)} async-done(((bf16[240,2560]{1,0:T(8,128)(2,1)}), bf16[960,2560]{1,0:T(8,128)(2,1)}) %all-gather.14.cloned.1.call-update) | async-done | bytes 4915216 | tf_op jit(solution)/shard_map/all_gather | solution.py:195
  214.3 7.0 fusion.40
  221.3 53.4 %all-gather.12.cloned.1.call-done = bf16[960,2560]{1,0:T(8,128)(2,1)} async-done(((bf16[240,2560]{1,0:T(8,128)(2,1)}), bf16[960,2560]{1,0:T(8,128)(2,1)}) %all-gather.12.cloned.1.call-update) | async-done | bytes 4915216 | tf_op jit(solution)/shard_map/all_gather | solution.py:194
  274.7 7.1 fusion.39
  281.8 53.4 %all-gather.16.cloned.1.call-done = bf16[2560,960]{0,1:T(8,128)(2,1)} async-done(((bf16[640,960]{0,1:T(8,128)(2,1)}), bf16[2560,960]{0,1:T(8,128)(2,1)}) %all-gather.16.cloned.1.call-update) | async-done | bytes 4915216 | tf_op jit(solution)/shard_map/all_gather | solution.py:196
  335.2 10.8 %multiply_convert_fusion = (bf16[512,2560]{1,0:T(8,128)(2,1)S(1)}, bf16[512,2560]{1,0:T(8,128)(2,1)S(1)}, bf16[512,2560]{1,0:T(8,128)(2,1)}) fusion(f32[512,2560]{1,0:T(8,128)} %fusion.39, f32[512,2560]{1,0:T(8,128)} %fusion.40, bf16[2560,960]{0,1:T(8,128)(2,1)} %all-gather.16.cloned.1.call-done, bf16[1,512,960]{1,2,0:T(8,128)(2,1)} %param.19), kind=kOutput, calls=%fused_computation.3 | convolution fusion | flops 2537553920 | bytes 24248320 | tf_op jit(solution)/shard_map/td,fd->tf/dot_general | solution.py:251
  346.0 2.7 fusion.41
  348.8 6.1 multiply_reduce_fusion
  356.5 2.1 fusion.14.doT
  358.6 40.8 %attn_bwd.1 = (f32[960,512]{1,0:T(8,128)}, bf16[8,640,512]{2,1,0:T(8,128)(2,1)}) custom-call(s32[2]{0:T(128)} %get-tuple-element.33.qblk, s32[16]{0:T(128)} %all-reduce.kblk, s32[1]{0:T(128)} %bitcast.3.own, bf16[960,512]{1,0:T(8,128)(2,1)} %bitcast.103, bf16[8,640,512]{2,1,0:T(8,128)(2,1)} %bitcast.101, bf16[960,512]{1,0:T(8,128)(2,1)} %get-tuple-element.13.oT, ...), custom_call_target="tpu_custom_call" | custom-call | tf_op jit(solution)/shard_map/attn_bwd/pallas_call | solution.py:185
  399.8 6.9 convolution_convert_fusion
  406.7 7.8 copy.19
  414.6 4.4 convolution_convert_fusion.4
  419.1 6.1 convolution_convert_fusion.1
  425.3 6.1 convolution_convert_fusion.2
  431.5 1.8 broadcast_multiply_fusion
  433.7 1.3 copy-done
  435.1 1.5 fusion.3
  436.5 22.9 %reduce-scatter.11.cloned.1.call-done = bf16[1,640,512]{2,1,0:T(8,128)(2,1)} async-done(((bf16[8,640,512]{2,1,0:T(8,128)(2,1)}), bf16[1,640,512]{2,1,0:T(8,128)(2,1)}) %reduce-scatter.11.cloned.1.call-update) | async-done | bytes 655376 | tf_op jit(solution)/shard_map/reduce_scatter | solution.py:269
  462.4 3.7 convolution_convert_fusion.3
  466.2 56.1 %reduce-scatter.19.cloned.1.call-done = bf16[640,960]{1,0:T(8,128)(2,1)} async-done(((bf16[2560,960]{1,0:T(8,128)(2,1)}), bf16[640,960]{1,0:T(8,128)(2,1)}) %reduce-scatter.19.cloned.1.call-update) | async-done | bytes 1228816
  522.2 2.4 copy.20
  524.6 35.4 %reduce-scatter.13.cloned.1.call-done = bf16[240,960]{1,0:T(8,128)(2,1)} async-done(((bf16[960,960]{1,0:T(8,128)(2,1)}), bf16[240,960]{1,0:T(8,128)(2,1)}) %reduce-scatter.13.cloned.1.call-update) | async-done | bytes 460816 | tf_op jit(solution)/shard_map/reduce_scatter | solution.py:303
  560.0 61.6 %reduce-scatter.17.cloned.1.call-done = bf16[240,2560]{1,0:T(8,128)(2,1)} async-done(((bf16[960,2560]{1,0:T(8,128)(2,1)}), bf16[240,2560]{1,0:T(8,128)(2,1)}) %reduce-scatter.17.cloned.1.call-update) | async-done | bytes 1228816 | tf_op jit(solution)/shard_map/reduce_scatter | solution.py:309
  621.6 61.8 %reduce-scatter.15.cloned.1.call-done = bf16[240,2560]{1,0:T(8,128)(2,1)} async-done(((bf16[960,2560]{1,0:T(8,128)(2,1)}), bf16[240,2560]{1,0:T(8,128)(2,1)}) %reduce-scatter.15.cloned.1.call-update) | async-done | bytes 1228816 | tf_op jit(solution)/shard_map/reduce_scatter | solution.py:306
  683.4 47.6 %reduce-scatter.21.cloned.1.call-done = bf16[240,1600]{1,0:T(8,128)(2,1)} async-done(((bf16[960,1600]{1,0:T(8,128)(2,1)}), bf16[240,1600]{1,0:T(8,128)(2,1)}) %reduce-scatter.21.cloned.1.call-update) | async-done | bytes 768016
  731.6 7.0 fusion.15
  738.7 3.4 fusion.13
  742.1 8.9 %all-reduce.8 = (bf16[960]{0:T(1024)(128)(2,1)S(1)}, bf16[960]{0:T(1024)(128)(2,1)S(1)}) all-reduce(bf16[960]{0:T(1024)(128)(2,1)S(1)} %get-tuple-element.19, bf16[960]{0:T(1024)(128)(2,1)S(1)} %copy-done.16), channel_id=9, replica_groups=mesh['dp'=4,'ctx'=8] {'dp'}, use_global_device_ids=true, to_apply=%region_16.17.clone | all-reduce | flops 1920 | bytes 7680
  751.2 15.6 %all-reduce.6 = (bf16[240]{0:T(256)(128)(2,1)S(1)}, bf16[240]{0:T(256)(128)(2,1)S(1)}) all-reduce(bf16[240]{0:T(256)(128)(2,1)S(1)} %dynamic-slice.6, bf16[240]{0:T(256)(128)(2,1)S(1)} %dynamic-slice.8), channel_id=1, replica_groups=mesh['dp'=4,'ctx'=8] {'ctx'}, use_global_device_ids=true, to_apply=%region_17.18 | all-reduce | flops 480 | bytes 1920 | tf_op jit(solution)/shard_map/psum | solution.py:328
  767.9 3.0 fusion.16
  770.9 76.8 %all-reduce.12.cloned.1.call-done = (bf16[240,1600]{1,0:T(8,128)(2,1)}, bf16[240,960]{1,0:T(8,128)(2,1)}, bf16[240,2560]{1,0:T(8,128)(2,1)}, bf16[240,2560]{1,0:T(8,128)(2,1)}, bf16[640,960]{0,1:T(8,128)(2,1)}) async-done(((bf16[240,1600]{1,0:T(8,128)(2,1)}, bf16[240,960]{1,0:T(8,128)(2,1)}, bf16[240,2560]{1,0:T(8,128)(2,1)}, bf16[240,2560]{1,0:T(8,128)(2,1)}, bf16[640,960]{0,1:T(8,128)(2,1)}), ...) | async-done | bytes 4915216 | tf_op jit(solution)/shard_map/psum | solution.py:323
  847.7 2.5 convert_element_type.153
  851.2 1.7 convert_element_type.157
  853.0 1.7 convert_element_type.159
  854.7 1.6 convert_element_type.161
  (109 shorter events, 19.1 us)
Async XLA Ops:
  7.2 49.8 %all-gather.8.cloned.1.call-start = ((), (), s32[]{:S(2)}) async-start(), calls=%async_computation.6 | async-start | bytes 3993600 | tf_op jit(solution)/shard_map/all_gather | solution.py:192
  7.9 111.0 %all-gather.18.cloned.1.call-start = ((), (), s32[]{:S(2)}) async-start(), calls=%async_computation.15 | async-start | bytes 5898240 | tf_op jit(solution)/shard_map/all_gather | solution.py:226
  62.6 91.3 %all-gather.10.cloned.1.call-start = ((), (), s32[]{:S(2)}) async-start(), calls=%async_computation.7 | async-start | bytes 2457600 | tf_op jit(solution)/shard_map/all_gather | solution.py:193
  63.3 3.1 copy-start.19
  63.3 151.0 %all-gather.14.cloned.1.call-start = ((), (), s32[]{:S(2)}) async-start(), calls=%async_computation.9 | async-start | bytes 6144000 | tf_op jit(solution)/shard_map/all_gather | solution.py:195
  63.9 210.8 %all-gather.12.cloned.1.call-start = ((), (), s32[]{:S(2)}) async-start(), calls=%async_computation.8 | async-start | bytes 6144000 | tf_op jit(solution)/shard_map/all_gather | solution.py:194
  64.5 270.7 %all-gather.16.cloned.1.call-start = ((), (), s32[]{:S(2)}) async-start(), calls=%async_computation.10 | async-start | bytes 6144000 | tf_op jit(solution)/shard_map/all_gather | solution.py:196
  65.0 394.4 %reduce-scatter.11.cloned.1.call-start = ((), (), s32[]{:S(2)}) async-start(), calls=%async_computation.11 | async-start | bytes 5898240 | tf_op jit(solution)/shard_map/reduce_scatter | solution.py:269
  118.9 35.0 %copy-start.4 = (bf16[1,512,960]{1,2,0:T(8,128)(2,1)S(1)}, bf16[1,512,960]{1,2,0:T(8,128)(2,1)}, u32[]{:S(2)}) copy-start(bf16[1,512,960]{1,2,0:T(8,128)(2,1)} %param.10) | copy-start | bytes 2949124
  335.2 10.9 %copy-start.3 = (bf16[960,2560]{1,0:T(8,128)(2,1)S(1)}, bf16[960,2560]{1,0:T(8,128)(2,1)}, u32[]{:S(2)}) copy-start(bf16[960,2560]{1,0:T(8,128)(2,1)} %all-gather.12.cloned.1.call-done) | copy-start | bytes 14745604
  346.0 2.8 copy-start.20
  346.0 2.8 copy-start.21
  348.8 6.1 copy-start.10
  354.9 1.5 copy-start.18
  356.5 2.2 copy-start.1
  399.5 122.8 %reduce-scatter.19.cloned.1.call-start = ((), (), s32[]{:S(2)}) async-start(), calls=%async_computation.16 | async-start | bytes 6553600
  414.6 145.4 %reduce-scatter.13.cloned.1.call-start = ((), (), s32[]{:S(2)}) async-start(), calls=%async_computation.12 | async-start | bytes 2457600 | tf_op jit(solution)/shard_map/reduce_scatter | solution.py:303
  419.1 202.6 %reduce-scatter.17.cloned.1.call-start = ((), (), s32[]{:S(2)}) async-start(), calls=%async_computation.14 | async-start | bytes 6144000 | tf_op jit(solution)/shard_map/reduce_scatter | solution.py:309
  425.2 258.2 %reduce-scatter.15.cloned.1.call-start = ((), (), s32[]{:S(2)}) async-start(), calls=%async_computation.13 | async-start | bytes 6144000 | tf_op jit(solution)/shard_map/reduce_scatter | solution.py:306
  431.4 299.5 %reduce-scatter.21.cloned.1.call-start = ((), (), s32[]{:S(2)}) async-start(), calls=%async_computation.17 | async-start | bytes 3993600
  433.5 1.6 copy-start
  460.6 1.3 copy-start.14
  460.6 1.2 copy-start.6
  460.7 1.4 copy-start.5
  460.7 1.7 copy-start.11
  466.1 381.6 %all-reduce.12.cloned.1.call-start = ((), (), s32[]{:S(2)}) async-start(), calls=%async_computation.18 | async-start | bytes 9953280 | tf_op jit(solution)/shard_map/psum | solution.py:323
  731.6 7.0 copy-start.12
  731.6 7.0 copy-start.15
  731.6 7.0 copy-start.17
  738.7 3.4 copy-start.16
  738.7 29.2 %copy-start.2 = (f32[512,960]{0,1:T(8,128)S(1)}, f32[512,960]{0,1:T(8,128)}, u32[]{:S(2)}) copy-start(f32[512,960]{0,1:T(8,128)} %copy-done.1) | copy-start | bytes 5898244
  847.7 2.5 copy-start.13
  847.7 3.6 copy-start.9
  851.2 1.7 copy-start.8
  853.0 1.7 copy-start.7
Sparse Core Ops, SparseCore 0:
  9.9 47.0 all-gather.7
  62.7 56.1 all-gather.17
  120.7 33.0 all-gather.9
  155.6 58.6 all-gather.13
  216.0 58.6 all-gather.11
  276.4 58.6 all-gather.15
  399.6 59.7 reduce-scatter.10
  462.4 59.7 reduce-scatter.18
  525.9 34.0 reduce-scatter.12
  562.9 58.7 reduce-scatter.16
  624.7 58.7 reduce-scatter.14
  686.3 44.6 reduce-scatter.20
  734.5 113.0 all-reduce.11
